TPU v7x, 32 devices: a whole 2x2x4 slice. The times are simulated.
32 devices in a mesh: grp: 2 (over y), row: 4 (over x, core), col: 4 (over z).
Axes of the slice: x: 2, y: 2, z: 4, core: 2. Of those that a mesh axis runs over, the one named last changes fastest.
Arguments:
- video: bfloat16 [514, 32, 512], P('grp', 'row', 'col'), parts along dimension 0, may hold values from -6 to 6, as said below
- filters: float32 [4, 2, 7, 7], replicated, may hold values from -0.875 to 0.875
- start_basis: float32 [256, 64], replicated, may hold values from -6 to 6
Outputs:
- basis: float32 [512, 64], P('grp'), parts along dimension 0
- modes: float32 [16, 128, 256], P(('grp', 'row'), 'col'), parts along dimension 0
There are 2 independent parts, one for each index of `grp`. A program takes and returns all parts, laid end to end along the dimension named above; an argument that names none is the same for every part. Nothing has to cross between parts.
Inputs may be any that keep to these rules, and one draw needn't show every extreme that they name: `video`: grey levels: a fixed texture plus a per-pixel oscillation in time.
All inputs are finite; a program needn't handle non-finite values.
Results may differ from a plain program's by a relative error of at most 0.0034.
Values may be sent and summed in bfloat16 or wider, within the bound.
No kernel may reach another device: no remote copies, remote signals or barrier semaphores. Data moves between devices by JAX's collectives and lax.ppermute only.
A program may use at most 64 MiB of HBM per device.

v0:
```python
import jax
import jax.numpy as jnp
from jax import lax
from jax.sharding import PartitionSpec as P

FRAMES = 256
MODES = 64
ORIENT = 4
TAPS = 7
SWEEPS = 2


def padded_2(array, sides, width):
    for axis, dim in sides:
        size, length = (lax.axis_size(axis), array.shape[dim])
        up = [(i, (i + 1) % size) for i in range(size - 1)]
        down = [(j, i) for i, j in up]
        last = lax.slice_in_dim(array, length - width, length, axis=dim)
        first = lax.slice_in_dim(array, 0, width, axis=dim)
        before = lax.ppermute(last, axis, up)
        after = lax.ppermute(first, axis, down)
        array = jnp.concatenate([before, array, after], axis=dim)
    return array


def orthonormal(stacked):
    inner = jnp.dot(stacked.T, stacked, precision=lax.Precision.HIGHEST)
    factor = jnp.linalg.cholesky(inner)
    return lax.linalg.triangular_solve(
        factor, stacked, left_side=False, lower=True, transpose_a=True
    )


def on_device(video, filters, start_basis):
    tile_rows = video.shape[1]
    tile_cols = video.shape[2]
    padded = padded_2(video, (("row", 1), ("col", 2)), 3)

    def orient(taps):
        kernels = taps.reshape(2, 1, TAPS, TAPS)
        lifted = padded.astype(jnp.float32)[:, None]
        response = lax.conv_general_dilated(
            lifted, kernels, (1, 1), "VALID", precision=lax.Precision.HIGHEST
        )
        real_part = response[:, 0]
        imag_part = response[:, 1]
        prod_real = real_part[1:] * real_part[:-1] + imag_part[1:] * imag_part[:-1]
        prod_imag = imag_part[1:] * real_part[:-1] - real_part[1:] * imag_part[:-1]
        motion = prod_imag / jnp.sqrt(prod_real * prod_real + prod_imag * prod_imag + 1.0)
        pooled = motion.reshape(FRAMES, tile_rows // 4, 4, tile_cols // 4, 4).mean(axis=(2, 4))
        return pooled.astype(jnp.bfloat16)

    stacked = lax.map(orient, filters)
    flat = jnp.transpose(stacked, (1, 0, 2, 3)).reshape(FRAMES, -1)
    devices_all = lax.axis_size("row") * lax.axis_size("col")
    npix_all = flat.shape[1] * devices_all
    basis_now = start_basis
    local_gram = jnp.dot(flat, flat.T, preferred_element_type=jnp.float32)
    gram = lax.psum(local_gram, ("row", "col")) / npix_all
    for sweep in range(SWEEPS):
        basis_now = orthonormal(jnp.dot(gram, basis_now, precision=lax.Precision.HIGHEST))
    projected = jnp.dot(basis_now.astype(jnp.bfloat16).T, flat, preferred_element_type=jnp.float32)
    fields = projected.reshape(MODES, ORIENT, tile_rows // 4, tile_cols // 4)
    modes = jnp.transpose(fields, (2, 3, 1, 0)).reshape(
        tile_rows // 4, tile_cols // 4, ORIENT * MODES
    )
    return (basis_now, modes)


def solution(mesh):
    return jax.shard_map(
        on_device,
        mesh=mesh,
        in_specs=(P("grp", "row", "col"), P(), P()),
        out_specs=(P("grp", None), P(("grp", "row"), "col", None)),
        check_vma=False,
    )
```

profile of v0, /device:TPU:1, one launch (start us, length us, event | category | flops | bytes accessed | tf_op | source)
XLA Modules:
  0.0 571.4 jit_solution(12141925055525839283)
XLA Ops:
  7.2 1.5 copy.25
  8.8 4.5 collective-permute-start
  13.3 1.9 collective-permute-start.1
  15.2 1.7 collective-permute-done
  16.9 4.4 collective-permute-done.1
  21.4 3.2 collective-permute-start.2
  24.6 1.3 collective-permute-start.3
  25.9 3.4 collective-permute-done.3
  29.3 1.8 pad_maximum_fusion
  31.1 414.1 %while.10 = (s32[]{:T(128)}, bf16[4,256,2,32]{1,3,2,0:T(8,128)(2,1)S(1)}, bf16[257,14,134]{0,2,1:T(8,128)(2,1)}, f32[4,2,7,7]{3,1,2,0:T(2,128)}, s32[]{:T(128)}) while((s32[]{:T(128)}, bf16[4,256,2,32]{1,3,2,0:T(8,128)(2,1)S(1)}, bf16[257,14,134]{0,2,1:T(8,128)(2,1)}, f32[4,2,7,7]{3,1,2,0:T(2,128)}, s32[]{:T(128)}) %tuple.29), condition=%wide.region_2.3_spmd, body=%wide.region_0.2_spmd.sunk | while | flops 312647680 | bytes 15818389 | solution.py:53
  31.1 0.7 dynamic-slice_bitcast_fusion.2
  32.0 87.6 %fusion.42 = f32[257,2,8,128]{0,1,3,2:T(2,128)S(1)} fusion(f32[2,1,7,7]{1,0,3,2:T(2,128)S(1)} %copy.40, bf16[257,1,14,134]{0,3,2,1:T(8,128)(2,1)} %bitcast.71), kind=kOutput, calls=%fused_computation.clone.1 | convolution fusion | flops 309485568 | bytes 3070000 | tf_op jit(solution)/shard_map/while/body/eval_jaxpr/conv_general_dilated | solution.py:42
  119.6 13.7 %multiply_reduce_fusion.4 = (f32[256,8,128]{0,2,1:T(8,128)S(1)}, f32[256,8,128]{0,2,1:T(8,128)S(1)}) fusion(f32[257,2,8,128]{0,1,3,2:T(2,128)S(1)} %fusion.42), kind=kLoop, calls=%fused_computation.3.clone.1 | loop fusion | flops 1835008 | bytes 6291456 | tf_op jit(solution)/shard_map/while/body/eval_jaxpr/mul | solution.py:49
  134.6 0.7 dynamic-slice_bitcast_fusion.2
  135.5 87.6 %fusion.42 = f32[257,2,8,128]{0,1,3,2:T(2,128)S(1)} fusion(f32[2,1,7,7]{1,0,3,2:T(2,128)S(1)} %copy.40, bf16[257,1,14,134]{0,3,2,1:T(8,128)(2,1)} %bitcast.71), kind=kOutput, calls=%fused_computation.clone.1 | convolution fusion | flops 309485568 | bytes 3070000 | tf_op jit(solution)/shard_map/while/body/eval_jaxpr/conv_general_dilated | solution.py:42
  223.1 13.7 %multiply_reduce_fusion.4 = (f32[256,8,128]{0,2,1:T(8,128)S(1)}, f32[256,8,128]{0,2,1:T(8,128)S(1)}) fusion(f32[257,2,8,128]{0,1,3,2:T(2,128)S(1)} %fusion.42), kind=kLoop, calls=%fused_computation.3.clone.1 | loop fusion | flops 1835008 | bytes 6291456 | tf_op jit(solution)/shard_map/while/body/eval_jaxpr/mul | solution.py:49
  238.1 0.7 dynamic-slice_bitcast_fusion.2
  239.0 87.6 %fusion.42 = f32[257,2,8,128]{0,1,3,2:T(2,128)S(1)} fusion(f32[2,1,7,7]{1,0,3,2:T(2,128)S(1)} %copy.40, bf16[257,1,14,134]{0,3,2,1:T(8,128)(2,1)} %bitcast.71), kind=kOutput, calls=%fused_computation.clone.1 | convolution fusion | flops 309485568 | bytes 3070000 | tf_op jit(solution)/shard_map/while/body/eval_jaxpr/conv_general_dilated | solution.py:42
  326.6 13.7 %multiply_reduce_fusion.4 = (f32[256,8,128]{0,2,1:T(8,128)S(1)}, f32[256,8,128]{0,2,1:T(8,128)S(1)}) fusion(f32[257,2,8,128]{0,1,3,2:T(2,128)S(1)} %fusion.42), kind=kLoop, calls=%fused_computation.3.clone.1 | loop fusion | flops 1835008 | bytes 6291456 | tf_op jit(solution)/shard_map/while/body/eval_jaxpr/mul | solution.py:49
  341.6 0.7 dynamic-slice_bitcast_fusion.2
  342.5 87.6 %fusion.42 = f32[257,2,8,128]{0,1,3,2:T(2,128)S(1)} fusion(f32[2,1,7,7]{1,0,3,2:T(2,128)S(1)} %copy.40, bf16[257,1,14,134]{0,3,2,1:T(8,128)(2,1)} %bitcast.71), kind=kOutput, calls=%fused_computation.clone.1 | convolution fusion | flops 309485568 | bytes 3070000 | tf_op jit(solution)/shard_map/while/body/eval_jaxpr/conv_general_dilated | solution.py:42
  430.1 13.7 %multiply_reduce_fusion.4 = (f32[256,8,128]{0,2,1:T(8,128)S(1)}, f32[256,8,128]{0,2,1:T(8,128)S(1)}) fusion(f32[257,2,8,128]{0,1,3,2:T(2,128)S(1)} %fusion.42), kind=kLoop, calls=%fused_computation.3.clone.1 | loop fusion | flops 1835008 | bytes 6291456 | tf_op jit(solution)/shard_map/while/body/eval_jaxpr/mul | solution.py:49
  445.2 0.9 convolution_bitcast_fusion
  446.2 89.3 %all-reduce.2.cloned.1.call-done = f32[256,256]{1,0:T(8,128)} async-done(((f32[256,256]{1,0:T(8,128)}), f32[256,256]{1,0:T(8,128)}) %all-reduce.2.cloned.1.call-update) | async-done | bytes 262160 | tf_op jit(solution)/shard_map/psum | solution.py:59
  535.5 1.3 fusion.6
  537.2 5.8 %cholesky.44 = f32[64,64]{1,0:T(8,128)S(1)} custom-call(f32[64,64]{1,0:T(8,128)S(1)} %fusion.18), custom_call_target="Cholesky" | custom-call | tf_op jit(solution)/shard_map/jit(cholesky)/cholesky | solution.py:28
  543.7 0.7 fusion.12
  544.3 4.9 custom-call.6
  549.5 1.3 fusion.4
  551.1 5.8 %cholesky.55 = f32[64,64]{1,0:T(8,128)S(1)} custom-call(f32[64,64]{1,0:T(8,128)S(1)} %fusion.16), custom_call_target="Cholesky" | custom-call | tf_op jit(solution)/shard_map/jit(cholesky)/cholesky | solution.py:28
  558.3 4.9 custom-call.7
  563.8 0.8 reshape.57
  (45 shorter events, 9.2 us)
Async XLA Ops:
  7.2 528.4 %copy-start = (f32[256,64]{0,1:T(8,128)S(1)}, f32[256,64]{0,1:T(8,128)}, u32[]{:S(2)}) copy-start(f32[256,64]{0,1:T(8,128)} %param.10) | copy-start | bytes 196612
  7.2 528.3 %all-reduce.2.cloned.1.call-start = ((), (), s32[]{:S(2)}) async-start(), calls=%async_computation | async-start | bytes 524288 | tf_op jit(solution)/shard_map/psum | solution.py:59
  8.8 8.2 %collective-permute-start = (bf16[257,3,128]{0,2,1:T(8,128)(2,1)S(1)}, bf16[257,3,128]{0,2,1:T(8,128)(2,1)S(1)}, u32[]{:S(2)}, u32[]{:S(2)}) collective-permute-start(bf16[257,3,128]{0,2,1:T(8,128)(2,1)S(1)} %get-tuple-element.39), channel_id=1, source_target_pairs={{0,4},{4,8},{8,12},{1,5},{5,9},{9,13},{2,6},{6,10},{10,14},{3,7},{... | collective-permute-start | bytes 592136 | tf_op jit(solution)/shard_map/ppermute | solution.py:20
  13.3 8.0 %collective-permute-start.1 = (bf16[257,3,128]{0,2,1:T(8,128)(2,1)S(1)}, bf16[257,3,128]{0,2,1:T(8,128)(2,1)S(1)}, u32[]{:S(2)}, u32[]{:S(2)}) collective-permute-start(bf16[257,3,128]{0,2,1:T(8,128)(2,1)S(1)} %get-tuple-element.40), channel_id=1, source_target_pairs={{4,0},{8,4},{12,8},{5,1},{9,5},{13,9},{6,2},{10,6},{14,10},{7,3},{... | collective-permute-start | bytes 592136 | tf_op jit(solution)/shard_map/ppermute | solution.py:21
  21.4 4.5 collective-permute-start.2
  24.6 4.8 collective-permute-start.3
  563.5 1.0 copy-start.1
Sparse Core Ops, SparseCore 0:
  446.3 89.1 all-reduce.1
where the time goes:
time: 572 us; the launch traced here: 571 us
  matrix products  355 us (62%)
  waiting for transfers between devices  98.9 us (17%)
  other arithmetic  83.2 us (15%)
  between operations  14.2 us (2%)
  starting transfers between devices  11 us (2%)
  local copies, waits for them, and re-layouts  8.54 us (1%)
    conv_general_dilated x4, matrix products, orient(): lax.conv_general_dilated(lifted, kernels, (1, 1), 'VALID', precision=lax....  350 us
    psum x1, waiting for transfers between devices, on_device(): gram = lax.psum(local_gram, ('row', 'col')) / npix_all  89.3 us
    mul x4, other arithmetic, orient(): prod_real * prod_real + prod_imag * prod_imag + 1.0  54.8 us
    another operation x6, other arithmetic, orthonormal(): factor = jnp.linalg.cholesky(inner)  13 us
  transfers between devices with their start and end apart: 5, of which 4 were waited for; matrix products, arithmetic and copies ran while one was open for 0% of the time, Pallas kernels for 0%

commit v1 on v0

--- a/solution.py
+++ b/solution.py
@@ -56,7 +56,11 @@
     npix_all = flat.shape[1] * devices_all
     basis_now = start_basis
     local_gram = jnp.dot(flat, flat.T, preferred_element_type=jnp.float32)
-    gram = lax.psum(local_gram, ("row", "col")) / npix_all
+
+    def _press_series(arr, device_axis):
+        return lax.all_gather(arr, axis_name=device_axis).sum(axis=0)
+
+    gram = _press_series(local_gram, ("row", "col")) / npix_all
     for sweep in range(SWEEPS):
         basis_now = orthonormal(jnp.dot(gram, basis_now, precision=lax.Precision.HIGHEST))
     projected = jnp.dot(basis_now.astype(jnp.bfloat16).T, flat, preferred_element_type=jnp.float32)

time: 572 us -> 534 us (0.934)
  waiting for transfers between devices: 98.9 us -> 60.4 us
    psum x1 -> x0, waiting for transfers between devices: 89.3 us -> none  [on_device(): gram = lax.psum(local_gram, ('row', 'col')) / npix_all]
    all_gather x0 -> x1, waiting for transfers between devices: none -> 50.9 us  [_press_series(): return lax.all_gather(arr, axis_name=device_axis).sum(axis=0)]
where the time goes in v1:
time: 534 us
  matrix products  353 us (66%)
  other arithmetic  85.7 us (16%)
  waiting for transfers between devices  60.4 us (11%)
  between operations  14.2 us (3%)
  starting transfers between devices  11 us (2%)
  local copies, waits for them, and re-layouts  8.53 us (2%)
    conv_general_dilated x4, matrix products, orient(): lax.conv_general_dilated(lifted, kernels, (1, 1), 'VALID', precision=lax....  350 us
    mul x4, other arithmetic, orient(): prod_real * prod_real + prod_imag * prod_imag + 1.0  54.8 us
    all_gather x1, waiting for transfers between devices, _press_series(): return lax.all_gather(arr, axis_name=device_axis).sum(axis=0)  50.9 us
    another operation x6, other arithmetic, orthonormal(): factor = jnp.linalg.cholesky(inner)  13 us
    another operation x4, other arithmetic, orthonormal(): lax.linalg.triangular_solve(factor, stacked, left_side=False, lower=True,...  11.1 us
  transfers between devices with their start and end apart: 5, of which 4 were waited for; matrix products, arithmetic and copies ran while one was open for 0% of the time, Pallas kernels for 0%

profile of v1, /device:TPU:1, one launch (start us, length us, event | category | flops | bytes accessed | tf_op | source)
XLA Modules:
  0.0 533.5 jit_solution(459961156083617008)
XLA Ops:
  7.2 1.5 copy.25
  8.8 4.5 collective-permute-start
  13.3 1.9 collective-permute-start.1
  15.2 1.7 collective-permute-done
  16.9 4.4 collective-permute-done.1
  21.4 3.2 collective-permute-start.2
  24.6 1.3 collective-permute-start.3
  25.9 3.4 collective-permute-done.3
  29.3 1.8 pad_maximum_fusion
  31.1 414.1 %while.10 = (s32[]{:T(128)}, bf16[4,256,2,32]{1,3,2,0:T(8,128)(2,1)S(1)}, bf16[257,14,134]{0,2,1:T(8,128)(2,1)}, f32[4,2,7,7]{3,1,2,0:T(2,128)}, s32[]{:T(128)}) while((s32[]{:T(128)}, bf16[4,256,2,32]{1,3,2,0:T(8,128)(2,1)S(1)}, bf16[257,14,134]{0,2,1:T(8,128)(2,1)}, f32[4,2,7,7]{3,1,2,0:T(2,128)}, s32[]{:T(128)}) %tuple.29), condition=%wide.region_2.3_spmd, body=%wide.region_0.2_spmd.sunk | while | flops 312647680 | bytes 15818389 | solution.py:53
  31.1 0.7 dynamic-slice_bitcast_fusion.2
  32.0 87.6 %fusion.42 = f32[257,2,8,128]{0,1,3,2:T(2,128)S(1)} fusion(f32[2,1,7,7]{1,0,3,2:T(2,128)S(1)} %copy.40, bf16[257,1,14,134]{0,3,2,1:T(8,128)(2,1)} %bitcast.72), kind=kOutput, calls=%fused_computation.clone.1 | convolution fusion | flops 309485568 | bytes 3070000 | tf_op jit(solution)/shard_map/while/body/eval_jaxpr/conv_general_dilated | solution.py:42
  119.6 13.7 %multiply_reduce_fusion.4 = (f32[256,8,128]{0,2,1:T(8,128)S(1)}, f32[256,8,128]{0,2,1:T(8,128)S(1)}) fusion(f32[257,2,8,128]{0,1,3,2:T(2,128)S(1)} %fusion.42), kind=kLoop, calls=%fused_computation.3.clone.1 | loop fusion | flops 1835008 | bytes 6291456 | tf_op jit(solution)/shard_map/while/body/eval_jaxpr/mul | solution.py:49
  134.6 0.7 dynamic-slice_bitcast_fusion.2
  135.5 87.6 %fusion.42 = f32[257,2,8,128]{0,1,3,2:T(2,128)S(1)} fusion(f32[2,1,7,7]{1,0,3,2:T(2,128)S(1)} %copy.40, bf16[257,1,14,134]{0,3,2,1:T(8,128)(2,1)} %bitcast.72), kind=kOutput, calls=%fused_computation.clone.1 | convolution fusion | flops 309485568 | bytes 3070000 | tf_op jit(solution)/shard_map/while/body/eval_jaxpr/conv_general_dilated | solution.py:42
  223.1 13.7 %multiply_reduce_fusion.4 = (f32[256,8,128]{0,2,1:T(8,128)S(1)}, f32[256,8,128]{0,2,1:T(8,128)S(1)}) fusion(f32[257,2,8,128]{0,1,3,2:T(2,128)S(1)} %fusion.42), kind=kLoop, calls=%fused_computation.3.clone.1 | loop fusion | flops 1835008 | bytes 6291456 | tf_op jit(solution)/shard_map/while/body/eval_jaxpr/mul | solution.py:49
  238.1 0.7 dynamic-slice_bitcast_fusion.2
  239.0 87.6 %fusion.42 = f32[257,2,8,128]{0,1,3,2:T(2,128)S(1)} fusion(f32[2,1,7,7]{1,0,3,2:T(2,128)S(1)} %copy.40, bf16[257,1,14,134]{0,3,2,1:T(8,128)(2,1)} %bitcast.72), kind=kOutput, calls=%fused_computation.clone.1 | convolution fusion | flops 309485568 | bytes 3070000 | tf_op jit(solution)/shard_map/while/body/eval_jaxpr/conv_general_dilated | solution.py:42
  326.6 13.7 %multiply_reduce_fusion.4 = (f32[256,8,128]{0,2,1:T(8,128)S(1)}, f32[256,8,128]{0,2,1:T(8,128)S(1)}) fusion(f32[257,2,8,128]{0,1,3,2:T(2,128)S(1)} %fusion.42), kind=kLoop, calls=%fused_computation.3.clone.1 | loop fusion | flops 1835008 | bytes 6291456 | tf_op jit(solution)/shard_map/while/body/eval_jaxpr/mul | solution.py:49
  341.6 0.7 dynamic-slice_bitcast_fusion.2
  342.5 87.6 %fusion.42 = f32[257,2,8,128]{0,1,3,2:T(2,128)S(1)} fusion(f32[2,1,7,7]{1,0,3,2:T(2,128)S(1)} %copy.40, bf16[257,1,14,134]{0,3,2,1:T(8,128)(2,1)} %bitcast.72), kind=kOutput, calls=%fused_computation.clone.1 | convolution fusion | flops 309485568 | bytes 3070000 | tf_op jit(solution)/shard_map/while/body/eval_jaxpr/conv_general_dilated | solution.py:42
  430.1 13.7 %multiply_reduce_fusion.4 = (f32[256,8,128]{0,2,1:T(8,128)S(1)}, f32[256,8,128]{0,2,1:T(8,128)S(1)}) fusion(f32[257,2,8,128]{0,1,3,2:T(2,128)S(1)} %fusion.42), kind=kLoop, calls=%fused_computation.3.clone.1 | loop fusion | flops 1835008 | bytes 6291456 | tf_op jit(solution)/shard_map/while/body/eval_jaxpr/mul | solution.py:49
  445.2 0.9 convolution_bitcast_fusion
  446.2 50.9 %all-gather.3.cloned.1.call-done = f32[4096,256]{1,0:T(8,128)} async-done(((f32[256,256]{1,0:T(8,128)}), f32[4096,256]{1,0:T(8,128)}) %all-gather.3.cloned.1.call-update) | async-done | bytes 4194320 | tf_op jit(solution)/shard_map/all_gather | solution.py:61
  497.0 2.5 reduce_sum.18
  500.2 5.8 %cholesky.44 = f32[64,64]{1,0:T(8,128)S(1)} custom-call(f32[64,64]{1,0:T(8,128)S(1)} %fusion.18), custom_call_target="Cholesky" | custom-call | tf_op jit(solution)/shard_map/jit(cholesky)/cholesky | solution.py:28
  506.7 0.7 fusion.12
  507.4 4.9 custom-call.6
  513.2 5.8 %cholesky.55 = f32[64,64]{1,0:T(8,128)S(1)} custom-call(f32[64,64]{1,0:T(8,128)S(1)} %fusion.16), custom_call_target="Cholesky" | custom-call | tf_op jit(solution)/shard_map/jit(cholesky)/cholesky | solution.py:28
  519.8 0.7 fusion.13
  520.4 4.9 custom-call.7
  525.9 0.8 reshape.57
  (46 shorter events, 9.3 us)
Async XLA Ops:
  7.2 492.4 %copy-start = (f32[256,64]{0,1:T(8,128)S(1)}, f32[256,64]{0,1:T(8,128)}, u32[]{:S(2)}) copy-start(f32[256,64]{0,1:T(8,128)} %param.10) | copy-start | bytes 196612
  7.2 489.9 %all-gather.3.cloned.1.call-start = ((), (), s32[]{:S(2)}) async-start(), calls=%async_computation | async-start | bytes 4456448 | tf_op jit(solution)/shard_map/all_gather | solution.py:61
  8.8 8.2 %collective-permute-start = (bf16[257,3,128]{0,2,1:T(8,128)(2,1)S(1)}, bf16[257,3,128]{0,2,1:T(8,128)(2,1)S(1)}, u32[]{:S(2)}, u32[]{:S(2)}) collective-permute-start(bf16[257,3,128]{0,2,1:T(8,128)(2,1)S(1)} %get-tuple-element.39), channel_id=1, source_target_pairs={{0,4},{4,8},{8,12},{1,5},{5,9},{9,13},{2,6},{6,10},{10,14},{3,7},{... | collective-permute-start | bytes 592136 | tf_op jit(solution)/shard_map/ppermute | solution.py:20
  13.3 8.0 %collective-permute-start.1 = (bf16[257,3,128]{0,2,1:T(8,128)(2,1)S(1)}, bf16[257,3,128]{0,2,1:T(8,128)(2,1)S(1)}, u32[]{:S(2)}, u32[]{:S(2)}) collective-permute-start(bf16[257,3,128]{0,2,1:T(8,128)(2,1)S(1)} %get-tuple-element.40), channel_id=1, source_target_pairs={{4,0},{8,4},{12,8},{5,1},{9,5},{13,9},{6,2},{10,6},{14,10},{7,3},{... | collective-permute-start | bytes 592136 | tf_op jit(solution)/shard_map/ppermute | solution.py:21
  21.4 4.5 collective-permute-start.2
  24.6 4.8 collective-permute-start.3
  525.6 1.0 copy-start.1
Sparse Core Ops, SparseCore 0:
  446.3 50.6 all-gather.2
